TPU v7x, 32 devices: a whole 2x2x4 slice. The times are simulated.
32 devices in a mesh: freq: 2 (over core), dir: 4 (over y, x), ap: 4 (over z).
Axes of the slice: x: 2, y: 2, z: 4, core: 2. Of those that a mesh axis runs over, the one named last changes fastest.
Arguments:
- signal: bfloat16 [2, 16384, 2048], P(None, 'ap', ('freq', 'dir')), parts along dimension 2, may hold values from -6 to 6
- positions: int32 [2, 16384], P(None, 'ap'), may hold values from 0 to 255
- weights: bfloat16 [4, 2, 2, 2, 256, 256], replicated, may hold values from -0.1875 to 0.1875
- directions: int32 [2, 16, 4096], P(None, 'ap', 'dir'), may hold values from 0 to 255
Outputs:
- beams: bfloat16 [2, 16, 4096, 2048], P(None, 'ap', 'dir', 'freq'), parts along dimension 3
There are 2 independent parts, one for each index of `freq`. A program takes and returns all parts, laid end to end along the dimension named above; an argument that names none is the same for every part. Nothing has to cross between parts.
All inputs are finite; a program needn't handle non-finite values.
Results may differ from a plain program's by a relative error of at most 0.009.
Values may be sent and summed in bfloat16 or wider, within the bound.
A program may use at most 128 MiB of HBM per device.

v0:
```python
import math

import jax
import jax.numpy as jnp
from jax import lax
from jax.sharding import PartitionSpec as P

K = 256
EB = 256
GRID = 256
LEVELS = 4
ABOX = 16


def from_partner(x, axis, distance):
    return lax.ppermute(x, axis, [(i, i ^ 1 << distance) for i in range(lax.axis_size(axis))])


def wave_table(element_x_position, coord_y, side, factor):
    wavenumber_index = jnp.arange(side * side, dtype=jnp.int32)
    wave_x = wavenumber_index // side - side // 2
    wave_y = wavenumber_index % side - side // 2
    phase_int = jnp.mod(element_x_position[..., None] * wave_x + coord_y[..., None] * wave_y, GRID)
    angle_rad = phase_int.astype(jnp.float32) * (2.0 * math.pi / GRID)
    return (jnp.cos(angle_rad) * factor, jnp.sin(angle_rad) * factor)


def group_phase(per_box, side):
    tile_rows = 1 << per_box.bit_length() // 2
    tile_columns = per_box // tile_rows
    group_index = jnp.arange(per_box, dtype=jnp.int32)
    centre_x = group_index % tile_rows * (GRID // tile_rows)
    centre_y = group_index // tile_rows * (GRID // tile_columns)
    return wave_table(centre_x, centre_y, side, 1.0)


def leaf_products(boxes_data, element_x_position, coord_y, side):
    wavenumber_index = jnp.arange(side * side, dtype=jnp.int32)
    wave_x = wavenumber_index // side - side // 2
    wave_y = wavenumber_index % side - side // 2
    phase_int = jnp.mod(
        element_x_position[:, None, :] * wave_x[None, :, None]
        + coord_y[:, None, :] * wave_y[None, :, None],
        GRID,
    )
    angle_rad = phase_int.astype(jnp.float32) * (2.0 * math.pi / GRID)
    factor = 1.0 / math.sqrt(EB)
    cosine = (jnp.cos(angle_rad) * factor).astype(jnp.bfloat16)
    sine_part = (jnp.sin(angle_rad) * factor).astype(jnp.bfloat16)
    first_table = jnp.concatenate([cosine, -sine_part], 1)
    second_table = jnp.concatenate([sine_part, cosine], 1)
    first_out = jnp.einsum(
        "bke,bec->bkc", first_table, boxes_data[0], preferred_element_type=jnp.float32
    )
    second_out = jnp.einsum(
        "bke,bec->bkc", second_table, boxes_data[1], preferred_element_type=jnp.float32
    )
    total = first_out + second_out
    boxes_here = total.shape[0]
    return total.reshape(boxes_here, 2, K, total.shape[-1]).astype(jnp.bfloat16)


def direction_table(element_x_position, coord_y, side):
    cosine, sine_part = wave_table(element_x_position, coord_y, side, 1.0 / math.sqrt(K))
    row_real = jnp.stack([cosine, -sine_part], -2)
    row_imag = jnp.stack([sine_part, cosine], -2)
    return jnp.stack([row_real, row_imag], -4).astype(jnp.bfloat16)


def evaluate_parts(steer_table, coeff_part):
    outputs = []
    for part_out in range(2):
        outputs.append(
            jnp.einsum(
                "aqik,aikc->aqc",
                steer_table[:, part_out],
                coeff_part,
                preferred_element_type=jnp.float32,
            )
        )
    return jnp.stack(outputs, 0).astype(jnp.bfloat16)


def expand(level_pair):
    w_real = level_pair[:, 0]
    w_imag = level_pair[:, 1]
    upper_rows = jnp.stack([w_real, -w_imag], 1)
    lower_rows = jnp.stack([w_imag, w_real], 1)
    block_matrix = jnp.stack([upper_rows, lower_rows], 0).transpose(0, 3, 1, 2, 4)
    return block_matrix.reshape(2 * K, 4 * K)


def merge_children(block_matrix, child_low, child_high):
    count = child_low.shape[0]
    width_cols = child_low.shape[-1]
    low_part = jnp.einsum(
        "ij,pjc->pic",
        block_matrix[:, : 2 * K],
        child_low.reshape(count, 2 * K, width_cols),
        preferred_element_type=jnp.float32,
    )
    high_part = jnp.einsum(
        "ij,pjc->pic",
        block_matrix[:, 2 * K :],
        child_high.reshape(count, 2 * K, width_cols),
        preferred_element_type=jnp.float32,
    )
    return (low_part + high_part).reshape(count, 2, K, width_cols)


def local_level(coeffs, level_weights, stride):
    count = coeffs.shape[0]
    width_cols = coeffs.shape[-1]
    grouped_boxes = coeffs.reshape(count // (2 * stride), 2, stride, 2, K, width_cols)
    child_low = grouped_boxes[:, 0].reshape(-1, 2, K, width_cols)
    child_high = grouped_boxes[:, 1].reshape(-1, 2, K, width_cols)
    results = []
    for parity_out in range(2):
        product = merge_children(expand(level_weights[parity_out]), child_low, child_high)
        results.append(product.reshape(count // (2 * stride), stride, 2, K, width_cols))
    return jnp.stack(results, 1).reshape(count, 2, K, width_cols).astype(jnp.bfloat16)


def partner_level(coeffs, level_weights, which_bit):
    partner = from_partner(coeffs, "ap", which_bit)
    parity = lax.axis_index("ap") >> which_bit & 1
    chosen = lax.dynamic_index_in_dim(level_weights, parity, 0, keepdims=False)
    ordered = jnp.where(parity == 0, chosen, chosen[::-1])
    return merge_children(expand(ordered), coeffs, partner).astype(jnp.bfloat16)


def reduce_boxes(coeffs, per_box):
    side = math.isqrt(K)
    count = coeffs.shape[0]
    width_cols = coeffs.shape[-1]
    cosine, sine_part = group_phase(per_box, side)
    cosine = cosine[:, :, None]
    sine_part = sine_part[:, :, None]
    grouped_boxes = coeffs.reshape(count // per_box, per_box, 2, K, width_cols)
    real_in = grouped_boxes[:, :, 0].astype(jnp.float32)
    imag_in = grouped_boxes[:, :, 1].astype(jnp.float32)
    real_part = jnp.sum(real_in * cosine + imag_in * sine_part, axis=1)
    imag_part = jnp.sum(imag_in * cosine - real_in * sine_part, axis=1)
    summed = jnp.stack([real_part, imag_part], 1)
    return (summed * (1.0 / math.sqrt(per_box))).astype(jnp.bfloat16)


def element_positions_route(coeffs, weights, all_boxes):
    boxes_here = coeffs.shape[0]
    for level_id in range(LEVELS):
        stride = all_boxes >> level_id + 1
        if stride >= boxes_here:
            which_bit = (stride // boxes_here).bit_length() - 1
            coeffs = partner_level(coeffs, weights[level_id], which_bit)
        else:
            coeffs = local_level(coeffs, weights[level_id], stride)
    return reduce_boxes(coeffs, all_boxes // ABOX)


def local(signal, positions, weights, directions):
    side = math.isqrt(K)
    boxes_here = positions.shape[1] // EB
    cols_here = signal.shape[2]
    all_boxes = boxes_here * lax.axis_size("ap")
    boxes_data = signal.reshape(2, boxes_here, EB, cols_here)
    element_x_position = positions[0].reshape(boxes_here, EB)
    coord_y = positions[1].reshape(boxes_here, EB)
    coeffs = leaf_products(boxes_data, element_x_position, coord_y, side)
    summed = element_positions_route(coeffs, weights, all_boxes)
    steer_table = direction_table(directions[0], directions[1], side)
    return evaluate_parts(steer_table, lax.all_gather(summed, "dir", axis=3, tiled=True))


def solution(mesh):
    in_specs = (P(None, "ap", ("freq", "dir")), P(None, "ap"), P(), P(None, "ap", "dir"))
    out_specs = P(None, "ap", "dir", "freq")
    return jax.shard_map(local, mesh=mesh, in_specs=in_specs, out_specs=out_specs, check_vma=False)
```

profile of v0, /device:TPU:0, one launch (start us, length us, event | category | flops | bytes accessed | tf_op | source)
XLA Modules:
  0.0 525.2 jit_solution(3754954989614468527)
XLA Ops:
  7.5 16.2 %fusion.57 = bf16[16,256,256]{2,1,0:T(8,128)(2,1)S(1)} fusion(s32[256]{0:T(256)S(1)} %get-tuple-element.64, s32[16,256]{1,0:T(8,128)S(1)} %mul.322, s32[256]{0:T(256)S(1)} %get-tuple-element.65, s32[16,256]{1,0:T(8,128)S(1)} %mul.318), kind=kLoop, calls=%fused_computation.147 | loop fusion | flops 22020096 | bytes 2131968 | tf_op jit(solution)/shard_map/neg | solution.py:50
  23.7 17.5 %multiply_convert_fusion = (bf16[16,256,256]{2,1,0:T(8,128)(2,1)S(1)}, bf16[16,256,256]{2,1,0:T(8,128)(2,1)S(1)}) fusion(s32[256]{0:T(256)S(1)} %get-tuple-element.64, s32[16,256]{1,0:T(8,128)S(1)} %mul.322, s32[256]{0:T(256)S(1)} %get-tuple-element.65, s32[16,256]{1,0:T(8,128)S(1)} %mul.318), kind=kLoop, calls=%fused_computation.49 | loop fusion | flops 20971520 | bytes 4229120 | tf_op jit(solution)/shard_map/convert_element_type | solution.py:49
  45.7 4.1 collective-permute-start
  54.6 4.6 fusion.41
  59.3 171.3 %collective-permute-done = bf16[16,2,256,256]{3,2,1,0:T(8,128)(2,1)} collective-permute-done((bf16[16,2,256,256]{3,2,1,0:T(8,128)(2,1)}, bf16[16,2,256,256]{3,2,1,0:T(8,128)(2,1)}, u32[]{:S(2)}, u32[]{:S(2)}) %collective-permute-start) | collective-permute-done | bytes 4194336 | tf_op jit(solution)/shard_map/ppermute | solution.py:16
  230.6 6.7 %fusion.12 = bf16[16,512,256]{1,2,0:T(8,128)(2,1)} fusion(f32[16,256,512]{2,1,0:T(8,128)S(1)} %fusion.41, bf16[16,512,256]{2,1,0:T(8,128)(2,1)} %bitcast.10, bf16[512,1024]{1,0:T(8,128)(2,1)S(1)} %reshape.380), kind=kOutput, calls=%fused_computation.28 | convolution fusion | flops 2151677952 | bytes 17301504 | tf_op jit(solution)/shard_map/ij,pjc->pic/dot_general | solution.py:102
  237.3 6.9 %convert_element_type.109 = bf16[16,2,256,256]{2,1,3,0:T(2,128)(2,1)} reshape(bf16[16,512,256]{1,2,0:T(8,128)(2,1)} %fusion.12) | data formatting | bytes 8388608 | tf_op jit(solution)/shard_map/convert_element_type | solution.py:129
  262.8 8.0 %fusion.40 = f32[16,256,512]{2,1,0:T(8,128)} fusion(bf16[16,512,256]{1,2,0:T(8,128)(2,1)} %fusion.12, bf16[512,1024]{1,0:T(8,128)(2,1)S(1)} %reshape.382), kind=kOutput, calls=%fused_computation.85 | convolution fusion | flops 2147483648 | bytes 13107200 | tf_op jit(solution)/shard_map/ij,pjc->pic/dot_general | solution.py:96
  270.8 65.6 %collective-permute-done.1 = bf16[16,2,256,256]{2,1,3,0:T(2,128)(2,1)} collective-permute-done((bf16[16,2,256,256]{2,1,3,0:T(2,128)(2,1)}, bf16[16,2,256,256]{2,1,3,0:T(2,128)(2,1)}, u32[]{:S(2)}, u32[]{:S(2)}) %collective-permute-start.1) | collective-permute-done | bytes 4194336 | tf_op jit(solution)/shard_map/ppermute | solution.py:16
  336.3 7.6 %reshape.383 = bf16[16,512,256]{1,2,0:T(8,128)(2,1)} reshape(bf16[16,2,256,256]{2,1,3,0:T(2,128)(2,1)} %collective-permute-done.1) | data formatting | bytes 8388608 | tf_op jit(solution)/shard_map/reshape | solution.py:105
  343.9 9.1 %fusion.13 = bf16[16,512,256]{1,2,0:T(8,128)(2,1)} fusion(f32[16,256,512]{2,1,0:T(8,128)} %fusion.40, bf16[16,512,256]{1,2,0:T(8,128)(2,1)} %reshape.383, bf16[512,1024]{1,0:T(8,128)(2,1)S(1)} %reshape.382), kind=kOutput, calls=%fused_computation.29 | convolution fusion | flops 2151677952 | bytes 17301504 | tf_op jit(solution)/shard_map/ij,pjc->pic/dot_general | solution.py:102
  353.0 6.9 %convert_element_type.112 = bf16[1,2,8,2,256,256]{4,3,5,2,1,0:T(2,128)(2,1)} reshape(bf16[16,512,256]{1,2,0:T(8,128)(2,1)} %fusion.13) | data formatting | bytes 8388608 | tf_op jit(solution)/shard_map/convert_element_type | solution.py:129
  359.9 6.0 %fusion.59 = (bf16[1,1,8,2,256,256]{4,3,5,2,1,0:T(2,128)(2,1)}, bf16[1,1,8,2,256,256]{4,3,5,2,1,0:T(2,128)(2,1)}) fusion(bf16[1,2,8,2,256,256]{4,3,5,2,1,0:T(2,128)(2,1)} %convert_element_type.112), kind=kLoop, calls=%fused_computation.149 | loop fusion | bytes 8388608 | tf_op jit(solution)/shard_map/slice | solution.py:116
  369.0 4.5 reshape_reshape_squeeze.16
  389.2 4.1 stack.162
  397.9 4.2 fusion.58
  405.3 4.4 reshape_reshape_squeeze.18
  415.3 4.2 copy.28
  425.1 4.0 copy.27
  434.3 20.1 %negate_convert_fusion = (bf16[4,1024,1,256]{3,1,2,0:T(8,128)(2,1)S(1)}, bf16[4,1024,1,256]{3,1,2,0:T(8,128)(2,1)}, bf16[4,1024,1,256]{3,1,2,0:T(8,128)(2,1)}) fusion(s32[256]{0:T(256)S(1)} %get-tuple-element.64, s32[4,1024]{1,0:T(4,128)S(1)} %get-tuple-element.57, s32[256]{0:T(256)S(1)} %get-tuple-element.65, s32[4,1024]{1,0:T(4,128)S(1)} %get-tuple-element.56), kind=kLoop, calls=%fused_computation.51 | loop fusion | flops 23068672 | bytes 6326272 | tf_op jit(solution)/shard_map/convert.25
  454.4 34.5 %all-gather.2.cloned.1.call-done = bf16[4,2,256,1024]{3,2,1,0:T(8,128)(2,1)} async-done(((bf16[4,2,256,256]{3,2,1,0:T(8,128)(2,1)}), bf16[4,2,256,1024]{3,2,1,0:T(8,128)(2,1)}) %all-gather.2.cloned.1.call-update) | async-done | bytes 4194320 | tf_op jit(solution)/shard_map/all_gather | solution.py:171
  488.9 8.0 %fusion.1 = bf16[1,4,1024,1024]{3,2,1,0:T(8,128)(2,1)S(1)} fusion(bf16[4,2,256,1024]{3,2,1,0:T(8,128)(2,1)} %all-gather.2.cloned.1.call-done, bf16[4,1024,1,256]{3,1,2,0:T(8,128)(2,1)} %get-tuple-element.53, bf16[4,1024,1,256]{3,1,2,0:T(8,128)(2,1)} %get-tuple-element.52), kind=kOutput, calls=%fused_computation.13 | convolution fusion | flops 4301258752 | bytes 16777216 | tf_op jit(solution)/shard_map/aqik,aikc->aqc/dot_general | solution.py:74
  496.9 10.6 %fusion = bf16[1,4,1024,1024]{3,2,1,0:T(8,128)(2,1)} fusion(bf16[4,2,256,1024]{3,2,1,0:T(8,128)(2,1)} %all-gather.2.cloned.1.call-done, bf16[4,1024,1,256]{3,1,2,0:T(8,128)(2,1)S(1)} %get-tuple-element.51, bf16[4,1024,1,256]{3,1,2,0:T(8,128)(2,1)} %get-tuple-element.53), kind=kOutput, calls=%fused_computation.12 | convolution fusion | flops 4301258752 | bytes 16777216 | tf_op jit(solution)/shard_map/aqik,aikc->aqc/dot_general | solution.py:74
  507.5 10.5 %pad_maximum_fusion = bf16[2,4,1024,1024]{3,2,1,0:T(8,128)(2,1)} fusion(bf16[1,4,1024,1024]{3,2,1,0:T(8,128)(2,1)S(1)} %fusion.1, bf16[1,4,1024,1024]{3,2,1,0:T(8,128)(2,1)} %fusion), kind=kLoop, calls=%fused_computation | loop fusion | flops 8388608 | bytes 33554432 | tf_op jit(solution)/shard_map/stack | solution.py:81
  (82 shorter events, 71.4 us)
Async XLA Ops:
  6.5 482.4 %all-gather.2.cloned.1.call-start = ((), (), s32[]{:S(2)}) async-start(), calls=%async_computation | async-start | bytes 5242880 | tf_op jit(solution)/shard_map/all_gather | solution.py:171
  7.5 33.7 %copy-start.2 = (bf16[2,4096,256]{2,1,0:T(8,128)(2,1)S(1)}, bf16[2,4096,256]{2,1,0:T(8,128)(2,1)}, u32[]{:S(2)}) copy-start(bf16[2,4096,256]{2,1,0:T(8,128)(2,1)} %param.4) | copy-start | bytes 12582916
  45.7 184.9 %collective-permute-start = (bf16[16,2,256,256]{3,2,1,0:T(8,128)(2,1)}, bf16[16,2,256,256]{3,2,1,0:T(8,128)(2,1)}, u32[]{:S(2)}, u32[]{:S(2)}) collective-permute-start(bf16[16,2,256,256]{3,2,1,0:T(8,128)(2,1)} %bitcast.9), channel_id=1, source_target_pairs={{0,2},{1,3},{2,0},{3,1},{4,6},{5,7},{6,4},{7,5},{8,10},{9,11},{10,... | collective-permute-start | bytes 12582920 | tf_op jit(solution)/shard_map/ppermute | solution.py:16
  244.3 92.1 %collective-permute-start.1 = (bf16[16,2,256,256]{2,1,3,0:T(2,128)(2,1)}, bf16[16,2,256,256]{2,1,3,0:T(2,128)(2,1)}, u32[]{:S(2)}, u32[]{:S(2)}) collective-permute-start(bf16[16,2,256,256]{2,1,3,0:T(2,128)(2,1)} %convert_element_type.109), channel_id=1, source_target_pairs={{0,1},{1,0},{2,3},{3,2},{4,5},{5,4},{6,7},{7,6},{8,9},{9,8},{10,11... | collective-permute-start | bytes 12582920 | tf_op jit(solution)/shard_map/ppermute | solution.py:16
  254.8 2.8 copy-start.7
  254.8 2.8 copy-start.8
  257.6 2.8 copy-start.6
  373.6 3.1 copy-start.4
  383.4 3.1 copy-start.5
  389.2 7.1 %copy-start = (bf16[1,2,4,2,256,256]{4,3,5,2,1,0:T(2,128)(2,1)S(1)}, bf16[1,2,4,2,256,256]{4,3,5,2,1,0:T(2,128)(2,1)}, u32[]{:S(2)}) copy-start(bf16[1,2,4,2,256,256]{4,3,5,2,1,0:T(2,128)(2,1)} %stack.168) | copy-start | bytes 6291460
  415.3 4.2 copy-start.3
  425.1 4.1 copy-start.1
  431.1 3.1 copy-start.9
Sparse Core Ops, SparseCore 0:
  434.4 54.4 all-gather.1
where the time goes:
time: 535 us; the launch traced here: 525 us
  waiting for transfers between devices  271 us (51%)
  local copies, waits for them, and re-layouts  87 us (16%)
  matrix products  74.1 us (14%)
  other arithmetic  73.7 us (14%)
  between operations  14.2 us (3%)
    ppermute x2, waiting for transfers between devices, from_partner(): lax.ppermute(x, axis, [(i, i ^ 1 << distance) for i in range(lax.axis_siz...  237 us
    all_gather x1, waiting for transfers between devices, local(): lax.all_gather(summed, 'dir', axis=3, tiled=True)  34.5 us
    dot_general x6, matrix products, merge_children(): jnp.einsum('ij,pjc->pic', block_matrix[:, 2 * K:], child_high.reshape(cou...  26.6 us
    dot_general x6, matrix products, merge_children(): jnp.einsum('ij,pjc->pic', block_matrix[:, :2 * K], child_low.reshape(coun...  24.7 us
    another operation x1, other arithmetic  20.1 us
    dot_general x2, matrix products, evaluate_parts(): jnp.einsum('aqik,aikc->aqc', steer_table[:, part_out], coeff_part, prefer...  18.6 us
    another operation x5, local copies, waits for them, and re-layouts, local_level(): jnp.stack(results, 1).reshape(count, 2, K, width_cols).astype(jnp.bfloat16)  17.9 us
    convert_element_type x1, other arithmetic, leaf_products(): sine_part = (jnp.sin(angle_rad) * factor).astype(jnp.bfloat16)  17.5 us
  transfers between devices with their start and end apart: 3, of which 3 were waited for; matrix products, arithmetic and copies ran while one was open for 10% of the time, Pallas kernels for 0%

commit v1 on v0

v1 whole, which is shorter than its diff:
```python
import functools
import math

import jax
import jax.numpy as jnp
from jax import lax
from jax.experimental import pallas as pl
from jax.experimental.pallas import tpu as pltpu
from jax.sharding import PartitionSpec as P

K = 256
EB = 256
GRID = 256
LEVELS = 4
ABOX = 16
SIDE = math.isqrt(K)
MESH = pl.DeviceIdType.MESH
MIB = 1 << 20


def log2(n):
    return n.bit_length() - 1


def dot(a, b):
    return jnp.dot(a, b, preferred_element_type=jnp.float32)


def classes(per_box):
    rx = 1 << per_box.bit_length() // 2
    return rx, per_box // rx


def wave_rows(x, y, factor):
    n = x.shape[-1]
    w = lax.broadcasted_iota(jnp.int32, (SIDE, n), 0) - SIDE // 2
    step = 2.0 * math.pi / GRID
    ax = ((w * x) & (GRID - 1)).astype(jnp.float32) * step
    ay = ((w * y) & (GRID - 1)).astype(jnp.float32) * step
    cx, sx = jnp.cos(ax)[:, None, :] * factor, jnp.sin(ax)[:, None, :] * factor
    cy, sy = jnp.cos(ay)[None, :, :], jnp.sin(ay)[None, :, :]
    c = (cx * cy - sx * sy).reshape(K, n).astype(jnp.bfloat16)
    s = (sx * cy + cx * sy).reshape(K, n).astype(jnp.bfloat16)
    return c, s


def to_natural(per_box):
    rx, ry = classes(per_box)
    hx, hy = SIDE // rx, SIDE // ry
    row = lax.broadcasted_iota(jnp.int32, (K, K), 0)
    col = lax.broadcasted_iota(jnp.int32, (K, K), 1)
    y_high = row & (hy - 1)
    x_high = (row >> log2(hy)) & (hx - 1)
    cls = row >> (log2(hx) + log2(hy))
    y_low = cls & (ry - 1)
    x_low = cls >> log2(ry)
    natural = (x_high * rx + x_low) * SIDE + y_high * ry + y_low
    return jnp.where(col == natural, 1.0, 0.0).astype(jnp.bfloat16)


def leaf_kernel(per_box, pos_ref, sig_ref, y_ref):
    rx, ry = classes(per_box)
    scale = 1.0 / math.sqrt(per_box)
    real, imag = [], []
    for m in range(per_box):
        c, s = wave_rows(pos_ref[0, 0, m : m + 1, :], pos_ref[1, 0, m : m + 1, :], 1.0 / math.sqrt(EB))
        sr = sig_ref[0, m * EB : (m + 1) * EB, :]
        si = sig_ref[1, m * EB : (m + 1) * EB, :]
        real.append(dot(c, sr) + dot(s, si))
        imag.append(dot(c, si) - dot(s, sr))
    for cls in range(per_box):
        wx, wy = cls // ry - SIDE // 2, cls % ry - SIDE // 2
        tr = ti = None
        for m in range(per_box):
            phase = (wx * (m % rx) * (GRID // rx) + wy * (m // rx) * (GRID // ry)) % GRID
            if phase * 4 % GRID == 0:
                cc, ss = ((1.0, 0.0), (0.0, 1.0), (-1.0, 0.0), (0.0, -1.0))[phase * 4 // GRID]
            else:
                cc, ss = math.cos(2 * math.pi * phase / GRID), math.sin(2 * math.pi * phase / GRID)
            for a, b in ((cc, ss),):
                r = [v * f for v, f in ((real[m], a), (imag[m], b)) if f != 0.0]
                i = [v * f for v, f in ((imag[m], a), (real[m], -b)) if f != 0.0]
                for v in r:
                    tr = v if tr is None else tr + v
                for v in i:
                    ti = v if ti is None else ti + v
        y_ref[cls, 0, 0:K, :] = (tr * scale).astype(jnp.bfloat16)
        y_ref[cls, 0, K : 2 * K, :] = (ti * scale).astype(jnp.bfloat16)


def cmul(a, b):
    r = dot(a[0], b[0]) - dot(a[1], b[1])
    i = dot(a[0], b[1]) + dot(a[1], b[0])
    return r.astype(jnp.bfloat16), i.astype(jnp.bfloat16)


def weights_kernel(per_box, nap, ap_ref, w_ref, v_ref, u_ref):
    nb = log2(nap)
    nloc = ABOX // nap
    kc = K // per_box
    ap = ap_ref[0]
    top = [None]
    for level in range(nb):
        c = (ap >> (nb - 1 - level)) & 1
        nxt = []
        for old in top:
            for r in range(2):
                w = (w_ref[level, r, c, 0], w_ref[level, r, c, 1])
                nxt.append(w if old is None else cmul(w, old))
        top = nxt
    for r, (re, im) in enumerate(top):
        v_ref[r, 0:K, 0:K] = re
        v_ref[r, 0:K, K:] = -im
        v_ref[r, K:, 0:K] = im
        v_ref[r, K:, K:] = re
    perm = to_natural(per_box)
    parts = {(0, 0): None}
    for level in range(nb, LEVELS):
        mats = {}
        for r in range(2):
            for c in range(2):
                w = (w_ref[level, r, c, 0], w_ref[level, r, c, 1])
                if level == LEVELS - 1:
                    w = tuple(dot(perm, part).astype(jnp.bfloat16) for part in w)
                mats[r, c] = w
        nxt = {}
        for (r0, c0), old in parts.items():
            for (r, c), w in mats.items():
                nxt[2 * r0 + r, 2 * c0 + c] = w if old is None else cmul(w, old)
        parts = nxt
    for (r, c), part in parts.items():
        re, im = (perm, jnp.zeros_like(perm)) if part is None else part
        for cls in range(per_box):
            rows = slice(cls * kc, (cls + 1) * kc)
            a, b = r * 2 * kc, c * 2 * K
            u_ref[cls, a : a + kc, b : b + K] = re[rows]
            u_ref[cls, a : a + kc, b + K : b + 2 * K] = -im[rows]
            u_ref[cls, a + kc : a + 2 * kc, b : b + K] = im[rows]
            u_ref[cls, a + kc : a + 2 * kc, b + K : b + 2 * K] = re[rows]


def exchange_kernel(
    per_box, nap, ndir, y_ref, v_ref, u_ref, z_ref,
    xs, acc, part, from_left, from_right,
    send_right, recv_right, send_left, recv_left, gather_send, gather_recv,
):
    nloc = ABOX // nap
    kc = K // per_box
    cols = y_ref.shape[-1]
    me = lax.axis_index("ap")
    col = lax.axis_index("dir")
    has_left, has_right = me > 0, me < nap - 1

    barrier = pltpu.get_barrier_semaphore()

    @pl.when(has_left)
    def _():
        pl.semaphore_signal(barrier, inc=1, device_id={"ap": me - 1}, device_id_type=MESH)

    @pl.when(has_right)
    def _():
        pl.semaphore_signal(barrier, inc=1, device_id={"ap": me + 1}, device_id_type=MESH)

    for p in range(1, ndir):
        pl.semaphore_signal(
            barrier, inc=1, device_id={"dir": lax.rem(col + p, ndir)}, device_id_type=MESH
        )

    on_line = has_left.astype(jnp.int32) + has_right.astype(jnp.int32)
    pl.semaphore_wait(barrier, ndir - 1 + on_line)

    def right_copy(dest, cls, slot):
        return pltpu.make_async_remote_copy(
            src_ref=part.at[dest, cls], dst_ref=from_left.at[dest, cls],
            send_sem=send_right.at[slot], recv_sem=recv_right.at[dest, cls],
            device_id={"ap": me + 1}, device_id_type=MESH,
        )

    def left_copy(dest, cls, slot):
        return pltpu.make_async_remote_copy(
            src_ref=part.at[dest, cls], dst_ref=from_right.at[dest, cls],
            send_sem=send_left.at[slot], recv_sem=recv_left.at[dest, cls],
            device_id={"ap": me - 1}, device_id_type=MESH,
        )

    def gather_copy(p, cls, sender):
        rows = pl.ds(pl.multiple_of(cls * kc, kc), kc)
        place = z_ref.at[sender, :, :, rows, :]
        return pltpu.make_async_remote_copy(
            src_ref=place, dst_ref=place,
            send_sem=gather_send.at[p, cls], recv_sem=gather_recv.at[sender, cls],
            device_id={"dir": lax.rem(col + p, ndir)}, device_id_type=MESH,
        )

    def finish(cls):
        acc[...] = part[me, cls].astype(jnp.float32)

        @pl.when(has_left)
        def _():
            right_copy(me, cls, 0).wait_recv()
            acc[...] += from_left[me, cls].astype(jnp.float32)

        @pl.when(has_right)
        def _():
            left_copy(me, cls, 0).wait_recv()
            acc[...] += from_right[me, cls].astype(jnp.float32)

        rows = pl.ds(pl.multiple_of(cls * kc, kc), kc)
        z_ref[col, :, :, rows, :] = acc[...].astype(jnp.bfloat16).reshape(nloc, 2, kc, cols)
        for p in range(1, ndir):
            gather_copy(p, cls, col).start()

    mirrored = me >= nap // 2
    low = jnp.where(mirrored, nap - 1 - me, me)
    extra = nap - 1 - 2 * low
    n_right, n_left = nap - 1 - me, me

    def step(t, carry):
        cls, q = t // nap, t % nap
        u = jnp.maximum(q - extra, 0)
        d = low - u // 2
        paired = jnp.where(u % 2 == 0, low - d, low + d)
        dest = jnp.where(q < extra, nap - 1 - q, paired)
        dest = jnp.where(mirrored, nap - 1 - dest, dest)
        going_right, going_left = dest > me, dest < me

        for c in range(nloc):
            xs[c * 2 * K : (c + 1) * 2 * K, :] = dot(v_ref[dest], y_ref[cls, c]).astype(jnp.bfloat16)
        acc[...] = dot(u_ref[cls], xs[...])

        @pl.when(going_right & has_left)
        def _():
            right_copy(dest, cls, 0).wait_recv()
            acc[...] += from_left[dest, cls].astype(jnp.float32)

        @pl.when(going_left & has_right)
        def _():
            left_copy(dest, cls, 0).wait_recv()
            acc[...] += from_right[dest, cls].astype(jnp.float32)

        part[dest, cls] = acc[...].astype(jnp.bfloat16)

        @pl.when(going_right)
        def _():
            number = cls * n_right + (nap - 1 - dest)

            @pl.when(number >= 2)
            def _():
                right_copy(dest, cls, number % 2).wait_send()

            right_copy(dest, cls, number % 2).start()

        @pl.when(going_left)
        def _():
            number = cls * n_left + dest

            @pl.when(number >= 2)
            def _():
                left_copy(dest, cls, number % 2).wait_send()

            left_copy(dest, cls, number % 2).start()

        @pl.when((q == nap - 1) & (cls > 0))
        def _():
            finish(cls - 1)

        return carry

    lax.fori_loop(0, per_box * nap, step, 0)
    finish(per_box - 1)
    for slot in range(2):
        @pl.when(has_right)
        def _():
            right_copy(0, 0, slot).wait_send()

        @pl.when(has_left)
        def _():
            left_copy(0, 0, slot).wait_send()

    for p in range(1, ndir):
        def drain(cls, carry, p=p):
            gather_copy(p, cls, col).wait_send()
            gather_copy(p, cls, lax.rem(col + p, ndir)).wait_recv()
            return carry

        lax.fori_loop(0, per_box, drain, 0)


def beam_kernel(per_box, dir_ref, z_ref, out_ref, zn):
    ndir = z_ref.shape[0]
    cols = z_ref.shape[-1]

    @pl.when(pl.program_id(1) == 0)
    def _():
        perm = to_natural(per_box)
        for d in range(ndir):
            for i in range(2):
                natural = lax.dot_general(
                    perm, z_ref[d, 0, i], (((0,), (0,)), ((), ())), preferred_element_type=jnp.float32
                )
                zn[i, :, d * cols : (d + 1) * cols] = natural.astype(jnp.bfloat16)

    c, s = wave_rows(dir_ref[0, 0, 0], dir_ref[1, 0, 0], 1.0 / math.sqrt(K))
    c, s = c.T, s.T
    out_ref[0, 0] = (dot(c, zn[0]) - dot(s, zn[1])).astype(jnp.bfloat16)
    out_ref[1, 0] = (dot(s, zn[0]) + dot(c, zn[1])).astype(jnp.bfloat16)


def local(nap, ndir, signal, positions, weights, directions):
    boxes = positions.shape[1] // EB
    cols = signal.shape[2]
    per_box = boxes * nap // ABOX
    nloc = ABOX // nap
    kc = K // per_box
    rows = nloc * 2 * kc
    bf16 = jnp.bfloat16
    vmem = pl.BlockSpec(memory_space=pltpu.VMEM)

    y = pl.pallas_call(
        functools.partial(leaf_kernel, per_box),
        grid=(nloc,),
        in_specs=[
            pl.BlockSpec((2, 1, per_box, EB), lambda g: (0, g, 0, 0)),
            pl.BlockSpec((2, per_box * EB, cols), lambda g: (0, g, 0)),
        ],
        out_specs=pl.BlockSpec((per_box, 1, 2 * K, cols), lambda g: (0, g, 0, 0)),
        out_shape=jax.ShapeDtypeStruct((per_box, nloc, 2 * K, cols), bf16),
        compiler_params=pltpu.CompilerParams(vmem_limit_bytes=48 * MIB),
        name="leaf",
    )(positions.reshape(2, nloc, per_box, EB), signal)

    v, u = pl.pallas_call(
        functools.partial(weights_kernel, per_box, nap),
        in_specs=[pl.BlockSpec(memory_space=pltpu.SMEM), vmem],
        out_specs=[vmem, vmem],
        out_shape=[
            jax.ShapeDtypeStruct((nap, 2 * K, 2 * K), bf16),
            jax.ShapeDtypeStruct((per_box, rows, nloc * 2 * K), bf16),
        ],
        compiler_params=pltpu.CompilerParams(vmem_limit_bytes=48 * MIB),
        name="weight_products",
    )(lax.axis_index("ap").reshape(1).astype(jnp.int32), weights)

    block = (nap, per_box, rows, cols)
    z = pl.pallas_call(
        functools.partial(exchange_kernel, per_box, nap, ndir),
        in_specs=[vmem] * 3,
        out_specs=vmem,
        out_shape=jax.ShapeDtypeStruct((ndir, nloc, 2, K, cols), bf16),
        scratch_shapes=[
            pltpu.VMEM((nloc * 2 * K, cols), bf16),
            pltpu.VMEM((rows, cols), jnp.float32),
            pltpu.VMEM(block, bf16),
            pltpu.VMEM(block, bf16),
            pltpu.VMEM(block, bf16),
            pltpu.SemaphoreType.DMA((2,)),
            pltpu.SemaphoreType.DMA((nap, per_box)),
            pltpu.SemaphoreType.DMA((2,)),
            pltpu.SemaphoreType.DMA((nap, per_box)),
            pltpu.SemaphoreType.DMA((ndir, per_box)),
            pltpu.SemaphoreType.DMA((ndir, per_box)),
        ],
        compiler_params=pltpu.CompilerParams(
            collective_id=0, has_side_effects=True, vmem_limit_bytes=58 * MIB
        ),
        name="exchange",
    )(y, v, u)

    qd = directions.shape[2]
    qb = min(256, qd)
    return pl.pallas_call(
        functools.partial(beam_kernel, per_box),
        grid=(nloc, qd // qb),
        in_specs=[
            pl.BlockSpec((2, 1, 1, 1, qb), lambda a, q: (0, a, q, 0, 0)),
            pl.BlockSpec((ndir, 1, 2, K, cols), lambda a, q: (0, a, 0, 0, 0)),
        ],
        out_specs=pl.BlockSpec((2, 1, qb, ndir * cols), lambda a, q: (0, a, q, 0)),
        out_shape=jax.ShapeDtypeStruct((2, nloc, qd, ndir * cols), bf16),
        scratch_shapes=[pltpu.VMEM((2, K, ndir * cols), bf16)],
        compiler_params=pltpu.CompilerParams(vmem_limit_bytes=48 * MIB),
        name="beams",
    )(directions.reshape(2, nloc, qd // qb, 1, qb), z)


def solution(mesh):
    in_specs = (P(None, "ap", ("freq", "dir")), P(None, "ap"), P(), P(None, "ap", "dir"))
    out_specs = P(None, "ap", "dir", "freq")
    fn = functools.partial(local, mesh.shape["ap"], mesh.shape["dir"])
    return jax.shard_map(fn, mesh=mesh, in_specs=in_specs, out_specs=out_specs, check_vma=False)
```

time: 535 us -> 144 us (0.27)
  the two profiles are of different devices: /device:TPU:0 before, /device:TPU:8 now
where the time goes in v1:
time: 144 us
  Pallas kernels  137 us (95%)
  local copies, waits for them, and re-layouts  7.07 us (5%)
    pallas_call x1, Pallas kernels, local(): pl.pallas_call(functools.partial(exchange_kernel, per_box, nap, ndir), in...  102 us
    pallas_call x1, Pallas kernels, local(): pl.pallas_call(functools.partial(beam_kernel, per_box), grid=(nloc, qd //...  18.3 us
    pallas_call x1, Pallas kernels, local(): pl.pallas_call(functools.partial(weights_kernel, per_box, nap), in_specs=...  8.77 us
    pallas_call x1, Pallas kernels, local(): pl.pallas_call(functools.partial(leaf_kernel, per_box), grid=(nloc,), in_...  7.77 us
    unnamed x6, local copies, waits for them, and re-layouts  5.47 us

profile of v1, /device:TPU:8, one launch (start us, length us, event | category | flops | bytes accessed | tf_op | source)
XLA Modules:
  0.0 143.9 jit_solution(15770924020247268629)
XLA Ops:
  0.0 0.8 reshape.10.pos_ref
  0.8 0.8 reshape.9.dir_ref
  1.6 7.8 %leaf.1.y_ref = bf16[4,4,512,256]{3,2,1,0:T(8,128)(2,1)S(1)} custom-call(s32[2,4,4,256]{3,2,1,0:T(4,128)S(1)} %reshape.10.pos_ref, bf16[2,4096,256]{2,1,0:T(8,128)(2,1)} %sig_ref.1), custom_call_target="tpu_custom_call" | custom-call | tf_op jit(solution)/shard_map/leaf/pallas_call | solution.py:319
  9.4 0.0 copy-start.1
  9.4 1.9 %copy-done.1 = bf16[4,4,512,256]{3,2,1,0:T(8,128)(2,1)} copy-done((bf16[4,4,512,256]{3,2,1,0:T(8,128)(2,1)}, bf16[4,4,512,256]{3,2,1,0:T(8,128)(2,1)S(1)}, u32[]{:S(2)}) %copy-start.1) | copy-done | bytes 4194328
  11.3 8.8 %weight_products.1 = (bf16[4,512,512]{2,1,0:T(8,128)(2,1)S(1)}, bf16[4,512,2048]{2,1,0:T(8,128)(2,1)}) custom-call(s32[1]{0:T(128)} %bitcast.ap_ref, bf16[4,2,2,2,256,256]{5,4,3,2,1,0:T(8,128)(2,1)} %w_ref.1), custom_call_target="tpu_custom_call" | custom-call | tf_op jit(solution)/shard_map/weight_products/pallas_call | solution.py:332
  20.1 0.0 copy-start.2
  20.1 1.4 copy-done.2
  21.5 102.0 %exchange.1.z_ref = bf16[4,4,2,256,256]{4,3,2,1,0:T(8,128)(2,1)} custom-call(bf16[4,4,512,256]{3,2,1,0:T(8,128)(2,1)} %copy-done.1, bf16[4,512,512]{2,1,0:T(8,128)(2,1)} %copy-done.2, bf16[4,512,2048]{2,1,0:T(8,128)(2,1)} %get-tuple-element.8.u_ref), custom_call_target="tpu_custom_call" | custom-call | tf_op jit(solution)/shard_map/exchange/pallas_call | solution.py:345
  123.4 0.0 copy-start
  123.4 2.2 %copy-done = bf16[4,4,2,256,256]{4,3,2,1,0:T(8,128)(2,1)S(1)} copy-done((bf16[4,4,2,256,256]{4,3,2,1,0:T(8,128)(2,1)S(1)}, bf16[4,4,2,256,256]{4,3,2,1,0:T(8,128)(2,1)}, u32[]{:S(2)}) %copy-start) | copy-done | bytes 4194328
  125.6 18.3 %beams.1 = bf16[2,4,1024,1024]{3,2,1,0:T(8,128)(2,1)} custom-call(s32[2,4,4,1,256]{4,3,2,1,0:T(1,128)S(1)} %reshape.9.dir_ref, bf16[4,4,2,256,256]{4,3,2,1,0:T(8,128)(2,1)S(1)} %copy-done), custom_call_target="tpu_custom_call" | custom-call | tf_op jit(solution)/shard_map/beams/pallas_call | solution.py:371
Async XLA Ops:
  9.4 1.9 %copy-start.1 = (bf16[4,4,512,256]{3,2,1,0:T(8,128)(2,1)}, bf16[4,4,512,256]{3,2,1,0:T(8,128)(2,1)S(1)}, u32[]{:S(2)}) copy-start(bf16[4,4,512,256]{3,2,1,0:T(8,128)(2,1)S(1)} %leaf.1.y_ref) | copy-start | bytes 12582916
  20.1 1.4 copy-start.2
  123.4 2.2 %copy-start = (bf16[4,4,2,256,256]{4,3,2,1,0:T(8,128)(2,1)S(1)}, bf16[4,4,2,256,256]{4,3,2,1,0:T(8,128)(2,1)}, u32[]{:S(2)}) copy-start(bf16[4,4,2,256,256]{4,3,2,1,0:T(8,128)(2,1)} %exchange.1.z_ref) | copy-start | bytes 12582916

commit v2 on v1

--- a/solution.py
+++ b/solution.py
@@ -16,6 +16,7 @@
 SIDE = math.isqrt(K)
 MESH = pl.DeviceIdType.MESH
 MIB = 1 << 20
+SLOTS = 3
 
 
 def log2(n):
@@ -63,7 +64,7 @@
     scale = 1.0 / math.sqrt(per_box)
     real, imag = [], []
     for m in range(per_box):
-        c, s = wave_rows(pos_ref[0, 0, m : m + 1, :], pos_ref[1, 0, m : m + 1, :], 1.0 / math.sqrt(EB))
+        c, s = wave_rows(pos_ref[0:1, m * EB : (m + 1) * EB], pos_ref[1:2, m * EB : (m + 1) * EB], 1.0 / math.sqrt(EB))
         sr = sig_ref[0, m * EB : (m + 1) * EB, :]
         si = sig_ref[1, m * EB : (m + 1) * EB, :]
         real.append(dot(c, sr) + dot(s, si))
@@ -94,7 +95,7 @@
     return r.astype(jnp.bfloat16), i.astype(jnp.bfloat16)
 
 
-def weights_kernel(per_box, nap, ap_ref, w_ref, v_ref, u_ref):
+def weights_kernel(per_box, nap, cuts, ap_ref, w_ref, v_ref, u_ref):
     nb = log2(nap)
     nloc = ABOX // nap
     kc = K // per_box
@@ -130,21 +131,25 @@
         parts = nxt
     for (r, c), part in parts.items():
         re, im = (perm, jnp.zeros_like(perm)) if part is None else part
+        each = nloc // cuts
         for cls in range(per_box):
             rows = slice(cls * kc, (cls + 1) * kc)
-            a, b = r * 2 * kc, c * 2 * K
-            u_ref[cls, a : a + kc, b : b + K] = re[rows]
-            u_ref[cls, a : a + kc, b + K : b + 2 * K] = -im[rows]
-            u_ref[cls, a + kc : a + 2 * kc, b : b + K] = im[rows]
-            u_ref[cls, a + kc : a + 2 * kc, b + K : b + 2 * K] = re[rows]
+            chunk = cls * cuts + r // each
+            a, b = r % each * 2 * kc, c * 2 * K
+            u_ref[chunk, a : a + kc, b : b + K] = re[rows]
+            u_ref[chunk, a : a + kc, b + K : b + 2 * K] = -im[rows]
+            u_ref[chunk, a + kc : a + 2 * kc, b : b + K] = im[rows]
+            u_ref[chunk, a + kc : a + 2 * kc, b + K : b + 2 * K] = re[rows]
 
 
 def exchange_kernel(
-    per_box, nap, ndir, y_ref, v_ref, u_ref, z_ref,
+    per_box, nap, ndir, cuts, qb, y_ref, v_ref, u_ref, dir_ref, z_ref, e_ref,
     xs, acc, part, from_left, from_right,
     send_right, recv_right, send_left, recv_left, gather_send, gather_recv,
 ):
     nloc = ABOX // nap
+    each = nloc // cuts
+    chunks = per_box * cuts
     kc = K // per_box
     cols = y_ref.shape[-1]
     me = lax.axis_index("ap")
@@ -183,9 +188,13 @@
             device_id={"ap": me - 1}, device_id_type=MESH,
         )
 
+    def spot(cls):
+        rows = pl.ds(pl.multiple_of(cls // cuts * kc, kc), kc)
+        return pl.ds(cls % cuts * each, each), rows
+
     def gather_copy(p, cls, sender):
-        rows = pl.ds(pl.multiple_of(cls * kc, kc), kc)
-        place = z_ref.at[sender, :, :, rows, :]
+        boxes, rows = spot(cls)
+        place = z_ref.at[sender, boxes, :, rows, :]
         return pltpu.make_async_remote_copy(
             src_ref=place, dst_ref=place,
             send_sem=gather_send.at[p, cls], recv_sem=gather_recv.at[sender, cls],
@@ -205,8 +214,8 @@
             left_copy(me, cls, 0).wait_recv()
             acc[...] += from_right[me, cls].astype(jnp.float32)
 
-        rows = pl.ds(pl.multiple_of(cls * kc, kc), kc)
-        z_ref[col, :, :, rows, :] = acc[...].astype(jnp.bfloat16).reshape(nloc, 2, kc, cols)
+        boxes, rows = spot(cls)
+        z_ref[col, boxes, :, rows, :] = acc[...].astype(jnp.bfloat16).reshape(each, 2, kc, cols)
         for p in range(1, ndir):
             gather_copy(p, cls, col).start()
 
@@ -214,6 +223,22 @@
     low = jnp.where(mirrored, nap - 1 - me, me)
     extra = nap - 1 - 2 * low
     n_right, n_left = nap - 1 - me, me
+
+    blocks = e_ref.shape[0]
+    per_dir = blocks // nloc
+    every = chunks * nap // blocks
+
+    def steer(b):
+        box, lanes = b // per_dir, pl.ds(pl.multiple_of(b % per_dir * qb, qb), qb)
+        tables = wave_rows(
+            dir_ref[0, pl.ds(box, 1), lanes], dir_ref[1, pl.ds(box, 1), lanes], 1.0 / math.sqrt(K)
+        )
+        perm = to_natural(per_box)
+        for i in range(2):
+            turned = lax.dot_general(
+                tables[i], perm, (((0,), (1,)), ((), ())), preferred_element_type=jnp.float32
+            )
+            e_ref[b, i] = turned.astype(jnp.bfloat16)
 
     def step(t, carry):
         cls, q = t // nap, t % nap
@@ -224,9 +249,13 @@
         dest = jnp.where(mirrored, nap - 1 - dest, dest)
         going_right, going_left = dest > me, dest < me
 
-        for c in range(nloc):
-            xs[c * 2 * K : (c + 1) * 2 * K, :] = dot(v_ref[dest], y_ref[cls, c]).astype(jnp.bfloat16)
-        acc[...] = dot(u_ref[cls], xs[...])
+        @pl.when(cls % cuts == 0)
+        def _():
+            for c in range(nloc):
+                x = dot(v_ref[dest], y_ref[cls // cuts, c])
+                xs[dest, c * 2 * K : (c + 1) * 2 * K, :] = x.astype(jnp.bfloat16)
+
+        acc[...] = dot(u_ref[cls], xs[dest])
 
         @pl.when(going_right & has_left)
         def _():
@@ -244,31 +273,35 @@
         def _():
             number = cls * n_right + (nap - 1 - dest)
 
-            @pl.when(number >= 2)
+            @pl.when(number >= SLOTS)
             def _():
-                right_copy(dest, cls, number % 2).wait_send()
-
-            right_copy(dest, cls, number % 2).start()
+                right_copy(dest, cls, number % SLOTS).wait_send()
+
+            right_copy(dest, cls, number % SLOTS).start()
 
         @pl.when(going_left)
         def _():
             number = cls * n_left + dest
 
-            @pl.when(number >= 2)
+            @pl.when(number >= SLOTS)
             def _():
-                left_copy(dest, cls, number % 2).wait_send()
-
-            left_copy(dest, cls, number % 2).start()
-
-        @pl.when((q == nap - 1) & (cls > 0))
+                left_copy(dest, cls, number % SLOTS).wait_send()
+
+            left_copy(dest, cls, number % SLOTS).start()
+
+        @pl.when((q == 1) & (cls > 0))
         def _():
             finish(cls - 1)
 
+        @pl.when(t % every == every - 1)
+        def _():
+            steer(t // every)
+
         return carry
 
-    lax.fori_loop(0, per_box * nap, step, 0)
-    finish(per_box - 1)
-    for slot in range(2):
+    lax.fori_loop(0, chunks * nap, step, 0)
+    finish(chunks - 1)
+    for slot in range(SLOTS):
         @pl.when(has_right)
         def _():
             right_copy(0, 0, slot).wait_send()
@@ -283,27 +316,20 @@
             gather_copy(p, cls, lax.rem(col + p, ndir)).wait_recv()
             return carry
 
-        lax.fori_loop(0, per_box, drain, 0)
-
-
-def beam_kernel(per_box, dir_ref, z_ref, out_ref, zn):
-    ndir = z_ref.shape[0]
+        lax.fori_loop(0, chunks, drain, 0)
+
+
+def beam_kernel(e_ref, z_ref, out_ref):
     cols = z_ref.shape[-1]
-
-    @pl.when(pl.program_id(1) == 0)
-    def _():
-        perm = to_natural(per_box)
-        for d in range(ndir):
+    blocks, qb = e_ref.shape[0], e_ref.shape[2]
+    for b in range(blocks):
+        c, s = e_ref[b, 0], e_ref[b, 1]
+        tables = jnp.concatenate([c, -s], 1), jnp.concatenate([s, c], 1)
+        for d in range(z_ref.shape[0]):
+            coeffs = z_ref[d, 0].reshape(2 * K, cols)
             for i in range(2):
-                natural = lax.dot_general(
-                    perm, z_ref[d, 0, i], (((0,), (0,)), ((), ())), preferred_element_type=jnp.float32
-                )
-                zn[i, :, d * cols : (d + 1) * cols] = natural.astype(jnp.bfloat16)
-
-    c, s = wave_rows(dir_ref[0, 0, 0], dir_ref[1, 0, 0], 1.0 / math.sqrt(K))
-    c, s = c.T, s.T
-    out_ref[0, 0] = (dot(c, zn[0]) - dot(s, zn[1])).astype(jnp.bfloat16)
-    out_ref[1, 0] = (dot(s, zn[0]) + dot(c, zn[1])).astype(jnp.bfloat16)
+                beams = dot(tables[i], coeffs).astype(jnp.bfloat16)
+                out_ref[i, 0, b * qb : (b + 1) * qb, d * cols : (d + 1) * cols] = beams
 
 
 def local(nap, ndir, signal, positions, weights, directions):
@@ -312,7 +338,8 @@
     per_box = boxes * nap // ABOX
     nloc = ABOX // nap
     kc = K // per_box
-    rows = nloc * 2 * kc
+    cuts = min(2, nloc)
+    rows = nloc // cuts * 2 * kc
     bf16 = jnp.bfloat16
     vmem = pl.BlockSpec(memory_space=pltpu.VMEM)
 
@@ -320,67 +347,71 @@
         functools.partial(leaf_kernel, per_box),
         grid=(nloc,),
         in_specs=[
-            pl.BlockSpec((2, 1, per_box, EB), lambda g: (0, g, 0, 0)),
+            pl.BlockSpec((2, per_box * EB), lambda g: (0, g)),
             pl.BlockSpec((2, per_box * EB, cols), lambda g: (0, g, 0)),
         ],
         out_specs=pl.BlockSpec((per_box, 1, 2 * K, cols), lambda g: (0, g, 0, 0)),
         out_shape=jax.ShapeDtypeStruct((per_box, nloc, 2 * K, cols), bf16),
-        compiler_params=pltpu.CompilerParams(vmem_limit_bytes=48 * MIB),
+        compiler_params=pltpu.CompilerParams(vmem_limit_bytes=60 * MIB),
         name="leaf",
-    )(positions.reshape(2, nloc, per_box, EB), signal)
+    )(positions, signal)
 
     v, u = pl.pallas_call(
-        functools.partial(weights_kernel, per_box, nap),
+        functools.partial(weights_kernel, per_box, nap, cuts),
         in_specs=[pl.BlockSpec(memory_space=pltpu.SMEM), vmem],
         out_specs=[vmem, vmem],
         out_shape=[
             jax.ShapeDtypeStruct((nap, 2 * K, 2 * K), bf16),
-            jax.ShapeDtypeStruct((per_box, rows, nloc * 2 * K), bf16),
+            jax.ShapeDtypeStruct((per_box * cuts, rows, nloc * 2 * K), bf16),
         ],
-        compiler_params=pltpu.CompilerParams(vmem_limit_bytes=48 * MIB),
+        compiler_params=pltpu.CompilerParams(vmem_limit_bytes=60 * MIB),
         name="weight_products",
     )(lax.axis_index("ap").reshape(1).astype(jnp.int32), weights)
 
-    block = (nap, per_box, rows, cols)
-    z = pl.pallas_call(
-        functools.partial(exchange_kernel, per_box, nap, ndir),
-        in_specs=[vmem] * 3,
-        out_specs=vmem,
-        out_shape=jax.ShapeDtypeStruct((ndir, nloc, 2, K, cols), bf16),
+    qd = directions.shape[2]
+    qb = min(256, qd)
+    per_dir = qd // qb
+    block = (nap, per_box * cuts, rows, cols)
+    z, e = pl.pallas_call(
+        functools.partial(exchange_kernel, per_box, nap, ndir, cuts, qb),
+        in_specs=[vmem] * 4,
+        out_specs=[vmem] * 2,
+        out_shape=[
+            jax.ShapeDtypeStruct((ndir, nloc, 2, K, cols), bf16),
+            jax.ShapeDtypeStruct((nloc * per_dir, 2, qb, K), bf16),
+        ],
         scratch_shapes=[
-            pltpu.VMEM((nloc * 2 * K, cols), bf16),
+            pltpu.VMEM((nap, nloc * 2 * K, cols), bf16),
             pltpu.VMEM((rows, cols), jnp.float32),
             pltpu.VMEM(block, bf16),
             pltpu.VMEM(block, bf16),
             pltpu.VMEM(block, bf16),
-            pltpu.SemaphoreType.DMA((2,)),
-            pltpu.SemaphoreType.DMA((nap, per_box)),
-            pltpu.SemaphoreType.DMA((2,)),
-            pltpu.SemaphoreType.DMA((nap, per_box)),
-            pltpu.SemaphoreType.DMA((ndir, per_box)),
-            pltpu.SemaphoreType.DMA((ndir, per_box)),
+            pltpu.SemaphoreType.DMA((SLOTS,)),
+            pltpu.SemaphoreType.DMA((nap, per_box * cuts)),
+            pltpu.SemaphoreType.DMA((SLOTS,)),
+            pltpu.SemaphoreType.DMA((nap, per_box * cuts)),
+            pltpu.SemaphoreType.DMA((ndir, per_box * cuts)),
+            pltpu.SemaphoreType.DMA((ndir, per_box * cuts)),
         ],
         compiler_params=pltpu.CompilerParams(
             collective_id=0, has_side_effects=True, vmem_limit_bytes=58 * MIB
         ),
         name="exchange",
-    )(y, v, u)
-
-    qd = directions.shape[2]
-    qb = min(256, qd)
+    )(y, v, u, directions)
+
+    group = min(2, per_dir)
     return pl.pallas_call(
-        functools.partial(beam_kernel, per_box),
-        grid=(nloc, qd // qb),
+        beam_kernel,
+        grid=(nloc, per_dir // group),
         in_specs=[
-            pl.BlockSpec((2, 1, 1, 1, qb), lambda a, q: (0, a, q, 0, 0)),
+            pl.BlockSpec((group, 2, qb, K), lambda a, q: (a * (per_dir // group) + q, 0, 0, 0)),
             pl.BlockSpec((ndir, 1, 2, K, cols), lambda a, q: (0, a, 0, 0, 0)),
         ],
-        out_specs=pl.BlockSpec((2, 1, qb, ndir * cols), lambda a, q: (0, a, q, 0)),
+        out_specs=pl.BlockSpec((2, 1, group * qb, ndir * cols), lambda a, q: (0, a, q, 0)),
         out_shape=jax.ShapeDtypeStruct((2, nloc, qd, ndir * cols), bf16),
-        scratch_shapes=[pltpu.VMEM((2, K, ndir * cols), bf16)],
-        compiler_params=pltpu.CompilerParams(vmem_limit_bytes=48 * MIB),
+        compiler_params=pltpu.CompilerParams(vmem_limit_bytes=60 * MIB),
         name="beams",
-    )(directions.reshape(2, nloc, qd // qb, 1, qb), z)
+    )(e, z)
 
 
 def solution(mesh):

time: 144 us -> 132 us (0.917)
  the two profiles are of different devices: /device:TPU:8 before, /device:TPU:0 now
where the time goes in v2:
time: 132 us
  Pallas kernels  132 us (100%)
    pallas_call x1, Pallas kernels, local(): pl.pallas_call(functools.partial(exchange_kernel, per_box, nap, ndir, cut...  98.8 us
    pallas_call x1, Pallas kernels, local(): pl.pallas_call(beam_kernel, grid=(nloc, per_dir // group), in_specs=[pl.B...  15.5 us
    pallas_call x1, Pallas kernels, local(): pl.pallas_call(functools.partial(weights_kernel, per_box, nap, cuts), in_...  8.78 us
    pallas_call x1, Pallas kernels, local(): pl.pallas_call(functools.partial(leaf_kernel, per_box), grid=(nloc,), in_...  8.54 us

profile of v2, /device:TPU:0, one launch (start us, length us, event | category | flops | bytes accessed | tf_op | source)
XLA Modules:
  0.0 131.6 jit_solution(10585916522514719455)
XLA Ops:
  0.0 8.5 %leaf.1.y_ref = bf16[4,4,512,256]{3,2,1,0:T(8,128)(2,1)} custom-call(s32[2,4096]{1,0:T(2,128)} %pos_ref.1, bf16[2,4096,256]{2,1,0:T(8,128)(2,1)} %sig_ref.1), custom_call_target="tpu_custom_call" | custom-call | tf_op jit(solution)/shard_map/leaf/pallas_call | solution.py:346
  8.5 8.8 %weight_products.1 = (bf16[4,512,512]{2,1,0:T(8,128)(2,1)}, bf16[8,256,2048]{2,1,0:T(8,128)(2,1)}) custom-call(s32[1]{0:T(128)} %bitcast.ap_ref, bf16[4,2,2,2,256,256]{5,4,3,2,1,0:T(8,128)(2,1)} %w_ref.1), custom_call_target="tpu_custom_call" | custom-call | tf_op jit(solution)/shard_map/weight_products/pallas_call | solution.py:359
  17.3 98.8 %exchange.1 = (bf16[4,4,2,256,256]{4,3,2,1,0:T(8,128)(2,1)}, bf16[16,2,256,256]{3,2,1,0:T(8,128)(2,1)}) custom-call(bf16[4,4,512,256]{3,2,1,0:T(8,128)(2,1)} %leaf.1.y_ref, bf16[4,512,512]{2,1,0:T(8,128)(2,1)} %get-tuple-element.9.v_ref, bf16[8,256,2048]{2,1,0:T(8,128)(2,1)} %get-tuple-element.10.u_ref, s32[2,4,1024]{2,1,0:T(4,128)} %dir_ref.1), custom_call_target="tpu_custom_call" | custom-call | tf_op jit(solution)/shard_map/exchange/pallas_call | solution.py:375
  116.1 15.5 %beams.1 = bf16[2,4,1024,1024]{3,2,1,0:T(8,128)(2,1)} custom-call(bf16[16,2,256,256]{3,2,1,0:T(8,128)(2,1)} %get-tuple-element.11.e_ref, bf16[4,4,2,256,256]{4,3,2,1,0:T(8,128)(2,1)} %get-tuple-element.12.z_ref), custom_call_target="tpu_custom_call" | custom-call | tf_op jit(solution)/shard_map/beams/pallas_call | solution.py:403

commit v3 on v2

--- a/solution.py
+++ b/solution.py
@@ -16,7 +16,7 @@
 SIDE = math.isqrt(K)
 MESH = pl.DeviceIdType.MESH
 MIB = 1 << 20
-SLOTS = 3
+SLOTS = 4
 
 
 def log2(n):
@@ -67,8 +67,10 @@
         c, s = wave_rows(pos_ref[0:1, m * EB : (m + 1) * EB], pos_ref[1:2, m * EB : (m + 1) * EB], 1.0 / math.sqrt(EB))
         sr = sig_ref[0, m * EB : (m + 1) * EB, :]
         si = sig_ref[1, m * EB : (m + 1) * EB, :]
-        real.append(dot(c, sr) + dot(s, si))
-        imag.append(dot(c, si) - dot(s, sr))
+        both = jnp.concatenate([c, s], 0)
+        with_real, with_imag = dot(both, sr), dot(both, si)
+        real.append(with_real[:K] + with_imag[K:])
+        imag.append(with_imag[:K] - with_real[K:])
     for cls in range(per_box):
         wx, wy = cls // ry - SIDE // 2, cls % ry - SIDE // 2
         tr = ti = None
@@ -95,11 +97,10 @@
     return r.astype(jnp.bfloat16), i.astype(jnp.bfloat16)
 
 
-def weights_kernel(per_box, nap, cuts, ap_ref, w_ref, v_ref, u_ref):
+def weight_products(per_box, nap, cuts, ap, w_ref, v_ref, u_ref):
     nb = log2(nap)
     nloc = ABOX // nap
     kc = K // per_box
-    ap = ap_ref[0]
     top = [None]
     for level in range(nb):
         c = (ap >> (nb - 1 - level)) & 1
@@ -110,10 +111,11 @@
                 nxt.append(w if old is None else cmul(w, old))
         top = nxt
     for r, (re, im) in enumerate(top):
-        v_ref[r, 0:K, 0:K] = re
-        v_ref[r, 0:K, K:] = -im
-        v_ref[r, K:, 0:K] = im
-        v_ref[r, K:, K:] = re
+        a = r * 2 * K
+        v_ref[a : a + K, 0:K] = re
+        v_ref[a : a + K, K:] = -im
+        v_ref[a + K : a + 2 * K, 0:K] = im
+        v_ref[a + K : a + 2 * K, K:] = re
     perm = to_natural(per_box)
     parts = {(0, 0): None}
     for level in range(nb, LEVELS):
@@ -131,26 +133,25 @@
         parts = nxt
     for (r, c), part in parts.items():
         re, im = (perm, jnp.zeros_like(perm)) if part is None else part
-        each = nloc // cuts
         for cls in range(per_box):
             rows = slice(cls * kc, (cls + 1) * kc)
-            chunk = cls * cuts + r // each
-            a, b = r % each * 2 * kc, c * 2 * K
-            u_ref[chunk, a : a + kc, b : b + K] = re[rows]
-            u_ref[chunk, a : a + kc, b + K : b + 2 * K] = -im[rows]
-            u_ref[chunk, a + kc : a + 2 * kc, b : b + K] = im[rows]
-            u_ref[chunk, a + kc : a + 2 * kc, b + K : b + 2 * K] = re[rows]
+            a, b = r * 2 * kc, c * 2 * K
+            u_ref[cls, a : a + kc, b : b + K] = re[rows]
+            u_ref[cls, a : a + kc, b + K : b + 2 * K] = -im[rows]
+            u_ref[cls, a + kc : a + 2 * kc, b : b + K] = im[rows]
+            u_ref[cls, a + kc : a + 2 * kc, b + K : b + 2 * K] = re[rows]
 
 
 def exchange_kernel(
-    per_box, nap, ndir, cuts, qb, y_ref, v_ref, u_ref, dir_ref, z_ref, e_ref,
-    xs, acc, part, from_left, from_right,
+    per_box, nap, ndir, cuts, qb, y_ref, w_ref, dir_ref, z_ref, e_ref,
+    v_ref, u_ref, xs, own, acc, part, from_left, from_right,
     send_right, recv_right, send_left, recv_left, gather_send, gather_recv,
 ):
     nloc = ABOX // nap
     each = nloc // cuts
     chunks = per_box * cuts
     kc = K // per_box
+    size = each * 2 * kc
     cols = y_ref.shape[-1]
     me = lax.axis_index("ap")
     col = lax.axis_index("dir")
@@ -171,6 +172,7 @@
             barrier, inc=1, device_id={"dir": lax.rem(col + p, ndir)}, device_id_type=MESH
         )
 
+    weight_products(per_box, nap, cuts, me, w_ref, v_ref, u_ref)
     on_line = has_left.astype(jnp.int32) + has_right.astype(jnp.int32)
     pl.semaphore_wait(barrier, ndir - 1 + on_line)
 
@@ -249,13 +251,20 @@
         dest = jnp.where(mirrored, nap - 1 - dest, dest)
         going_right, going_left = dest > me, dest < me
 
+        @pl.when((cls % cuts == 0) & (q == 0))
+        def _():
+            for c in range(nloc):
+                x = dot(v_ref[...], y_ref[cls // cuts, c]).astype(jnp.bfloat16)
+                for r in range(nap):
+                    xs[r, c * 2 * K : (c + 1) * 2 * K, :] = x[r * 2 * K : (r + 1) * 2 * K]
+
         @pl.when(cls % cuts == 0)
         def _():
-            for c in range(nloc):
-                x = dot(v_ref[dest], y_ref[cls // cuts, c])
-                xs[dest, c * 2 * K : (c + 1) * 2 * K, :] = x.astype(jnp.bfloat16)
-
-        acc[...] = dot(u_ref[cls], xs[dest])
+            total = dot(u_ref[cls // cuts], xs[dest])
+            for h in range(cuts):
+                own[dest, h] = total[h * size : (h + 1) * size]
+
+        acc[...] = own[dest, cls % cuts]
 
         @pl.when(going_right & has_left)
         def _():
@@ -293,9 +302,14 @@
         def _():
             finish(cls - 1)
 
-        @pl.when(t % every == every - 1)
-        def _():
-            steer(t // every)
+        if chunks % every == 0:
+            @pl.when(cls % every == every - 1)
+            def _():
+                steer(cls // every * nap + q)
+        else:
+            @pl.when(t % every == every - 1)
+            def _():
+                steer(t // every)
 
         return carry
 
@@ -322,14 +336,17 @@
 def beam_kernel(e_ref, z_ref, out_ref):
     cols = z_ref.shape[-1]
     blocks, qb = e_ref.shape[0], e_ref.shape[2]
-    for b in range(blocks):
-        c, s = e_ref[b, 0], e_ref[b, 1]
-        tables = jnp.concatenate([c, -s], 1), jnp.concatenate([s, c], 1)
-        for d in range(z_ref.shape[0]):
-            coeffs = z_ref[d, 0].reshape(2 * K, cols)
-            for i in range(2):
-                beams = dot(tables[i], coeffs).astype(jnp.bfloat16)
-                out_ref[i, 0, b * qb : (b + 1) * qb, d * cols : (d + 1) * cols] = beams
+    tables = []
+    for i in range(2):
+        for b in range(blocks):
+            c, s = e_ref[b, 0], e_ref[b, 1]
+            tables.append(jnp.concatenate([s, c] if i else [c, -s], 1))
+    tall = jnp.concatenate(tables, 0)
+    for d in range(z_ref.shape[0]):
+        beams = dot(tall, z_ref[d, 0].reshape(2 * K, cols)).astype(jnp.bfloat16)
+        for i in range(2):
+            rows = slice(i * blocks * qb, (i + 1) * blocks * qb)
+            out_ref[i, 0, :, d * cols : (d + 1) * cols] = beams[rows]
 
 
 def local(nap, ndir, signal, positions, weights, directions):
@@ -356,32 +373,23 @@
         name="leaf",
     )(positions, signal)
 
-    v, u = pl.pallas_call(
-        functools.partial(weights_kernel, per_box, nap, cuts),
-        in_specs=[pl.BlockSpec(memory_space=pltpu.SMEM), vmem],
-        out_specs=[vmem, vmem],
-        out_shape=[
-            jax.ShapeDtypeStruct((nap, 2 * K, 2 * K), bf16),
-            jax.ShapeDtypeStruct((per_box * cuts, rows, nloc * 2 * K), bf16),
-        ],
-        compiler_params=pltpu.CompilerParams(vmem_limit_bytes=60 * MIB),
-        name="weight_products",
-    )(lax.axis_index("ap").reshape(1).astype(jnp.int32), weights)
-
     qd = directions.shape[2]
     qb = min(256, qd)
     per_dir = qd // qb
     block = (nap, per_box * cuts, rows, cols)
     z, e = pl.pallas_call(
         functools.partial(exchange_kernel, per_box, nap, ndir, cuts, qb),
-        in_specs=[vmem] * 4,
+        in_specs=[vmem] * 3,
         out_specs=[vmem] * 2,
         out_shape=[
             jax.ShapeDtypeStruct((ndir, nloc, 2, K, cols), bf16),
             jax.ShapeDtypeStruct((nloc * per_dir, 2, qb, K), bf16),
         ],
         scratch_shapes=[
+            pltpu.VMEM((nap * 2 * K, 2 * K), bf16),
+            pltpu.VMEM((per_box, cuts * rows, nloc * 2 * K), bf16),
             pltpu.VMEM((nap, nloc * 2 * K, cols), bf16),
+            pltpu.VMEM((nap, cuts, rows, cols), jnp.float32),
             pltpu.VMEM((rows, cols), jnp.float32),
             pltpu.VMEM(block, bf16),
             pltpu.VMEM(block, bf16),
@@ -397,7 +405,7 @@
             collective_id=0, has_side_effects=True, vmem_limit_bytes=58 * MIB
         ),
         name="exchange",
-    )(y, v, u, directions)
+    )(y, weights, directions)
 
     group = min(2, per_dir)
     return pl.pallas_call(

time: 132 us -> 124 us (0.939)
  Pallas kernels: 132 us -> 123 us
    pallas_call x1 -> x0, Pallas kernels: 8.78 us -> none  [local(): pl.pallas_call(functools.partial(weights_kernel, per_box, nap, cuts), in_...]
where the time goes in v3:
time: 124 us; the launch traced here: 123 us
  Pallas kernels  123 us (99%)
    pallas_call x1, Pallas kernels, local(): pl.pallas_call(functools.partial(exchange_kernel, per_box, nap, ndir, cut...  99.4 us
    pallas_call x1, Pallas kernels, local(): pl.pallas_call(beam_kernel, grid=(nloc, per_dir // group), in_specs=[pl.B...  15.5 us
    pallas_call x1, Pallas kernels, local(): pl.pallas_call(functools.partial(leaf_kernel, per_box), grid=(nloc,), in_...  8.11 us

profile of v3, /device:TPU:0, one launch (start us, length us, event | category | flops | bytes accessed | tf_op | source)
XLA Modules:
  0.0 123.0 jit_solution(7036215386986200950)
XLA Ops:
  0.0 8.1 %leaf.1.y_ref = bf16[4,4,512,256]{3,2,1,0:T(8,128)(2,1)} custom-call(s32[2,4096]{1,0:T(2,128)} %pos_ref.1, bf16[2,4096,256]{2,1,0:T(8,128)(2,1)} %sig_ref.1), custom_call_target="tpu_custom_call" | custom-call | tf_op jit(solution)/shard_map/leaf/pallas_call | solution.py:363
  8.1 99.4 %exchange.1 = (bf16[4,4,2,256,256]{4,3,2,1,0:T(8,128)(2,1)}, bf16[16,2,256,256]{3,2,1,0:T(8,128)(2,1)}) custom-call(bf16[4,4,512,256]{3,2,1,0:T(8,128)(2,1)} %leaf.1.y_ref, bf16[4,2,2,2,256,256]{5,4,3,2,1,0:T(8,128)(2,1)} %w_ref.1, s32[2,4,1024]{2,1,0:T(4,128)} %dir_ref.1), custom_call_target="tpu_custom_call" | custom-call | tf_op jit(solution)/shard_map/exchange/pallas_call | solution.py:380
  107.5 15.5 %beams.1 = bf16[2,4,1024,1024]{3,2,1,0:T(8,128)(2,1)} custom-call(bf16[16,2,256,256]{3,2,1,0:T(8,128)(2,1)} %get-tuple-element.7.e_ref, bf16[4,4,2,256,256]{4,3,2,1,0:T(8,128)(2,1)} %get-tuple-element.8.z_ref), custom_call_target="tpu_custom_call" | custom-call | tf_op jit(solution)/shard_map/beams/pallas_call | solution.py:411
